TPU v7x, 256 devices: a whole 4x4x8 slice. The times are simulated.
256 devices in a mesh: seg: 4 (over x_lo, core), chan: 64 (over y, z, x_hi).
Axes of the slice: x: 4 (x_hi: 2, x_lo: 2; x = x_hi * 2 + x_lo), y: 4, z: 8, core: 2. Of those that a mesh axis runs over, the one named last changes fastest.
Arguments:
- spectra: float32 [4, 4, 8192, 1024], P('seg', None, 'chan'), may hold values from -6 to 6
- valid: int32 [4, 8192], P('seg', 'chan'), may hold values from 1 to 4
Outputs:
- stacked: float32 [2, 64, 128, 101, 128], P(None, 'chan', 'seg')
All inputs are finite; a program needn't handle non-finite values.
Results may differ from a plain program's by a relative error of at most 0.019.
Values may be sent and summed in bfloat16 or wider, within the bound.
A program may use at most 192 MiB of HBM per device.

v0:
```python
import math

import jax
import jax.numpy as jnp
from jax import lax
from jax.sharding import PartitionSpec as P

ROUNDS = 2
LAGS = 101


def passed_along(value, axis, steps):
    count = lax.axis_size(axis)
    pairs = [(source, (source + steps) % count) for source in range(count)]
    return lax.ppermute(value, axis, pairs)


def lag_table(freqs, lags):
    freq_ids = jnp.arange(freqs, dtype=jnp.int32)[:, None]
    lag_ids = jnp.arange(lags, dtype=jnp.int32)[None, :] - (lags - 1) // 2
    phase = jnp.mod(freq_ids * lag_ids, 2 * freqs).astype(jnp.float32) * (math.pi / freqs)
    return jnp.concatenate([jnp.cos(phase), -jnp.sin(phase)], 0).astype(jnp.bfloat16)


def correlate(own_rows, far_rows, table):
    half = own_rows.shape[-1] // 2
    own_real = own_rows[..., :half][:, :, :, :, None]
    own_imag = own_rows[..., half:][:, :, :, :, None]
    far_turned = jnp.swapaxes(far_rows, 2, 3)
    far_real = far_turned[:, :, :half, :][:, :, None, :, :]
    far_imag = far_turned[:, :, half:, :][:, :, None, :, :]
    real_part = jnp.sum(own_real * far_real + own_imag * far_imag, axis=(0, 1))
    imag_part = jnp.sum(own_imag * far_real - own_real * far_imag, axis=(0, 1))
    spectrum = jnp.concatenate([real_part, imag_part], 1).astype(jnp.bfloat16)
    return jnp.einsum("ikj,kl->ilj", spectrum, table, preferred_element_type=jnp.float32)


def local(spectra, valid):
    seg_dev, windows, block_size, width = spectra.shape
    freqs = width // 2
    groups = lax.axis_size("seg")
    row_share = block_size // groups
    window_ids = jnp.arange(windows, dtype=jnp.int32)[None, :, None]
    counts = valid.astype(jnp.float32)
    weight = (window_ids < valid[:, None, :]).astype(jnp.float32) / jnp.sqrt(counts)[:, None, :]
    weighted = spectra * weight[..., None]
    table = lag_table(freqs, LAGS)
    scale = 1.0 / math.sqrt(freqs * seg_dev * groups)
    partners = []
    for turn_index in range(ROUNDS):
        partners.append(
            passed_along(weighted.astype(jnp.bfloat16), "chan", -(turn_index + 1)).astype(
                weighted.dtype
            )
        )
    rounds_out = []
    for far_rows in partners:
        count = row_share * lax.axis_size("seg")
        pieces = []
        for offset in range(0, count, row_share):
            own_rows = lax.dynamic_slice_in_dim(weighted, offset, row_share, 2)
            pieces.append(correlate(own_rows, far_rows, table) * scale)
        rounds_out.append(
            lax.psum_scatter(
                jnp.concatenate(pieces, 0).astype(jnp.bfloat16),
                "seg",
                scatter_dimension=0,
                tiled=True,
            ).astype(jnp.float32)
        )
    stacked = jnp.stack(rounds_out, 0)
    return stacked[:, None]


def solution(mesh):
    return jax.shard_map(
        local,
        mesh=mesh,
        in_specs=(P("seg", None, "chan", None), P("seg", "chan")),
        out_specs=P(None, "chan", "seg", None, None),
        check_vma=False,
    )
```

profile of v0, /device:TPU:1, one launch (start us, length us, event | category | flops | bytes accessed | tf_op | source)
XLA Modules:
  0.0 326.9 jit_solution(8166665012813058937)
XLA Ops:
  6.5 0.0 reduce-scatter.5.cloned.1.call-start
  6.5 0.7 sqrt_bitcast_fusion
  7.2 0.7 convert_divide_fusion
  7.9 2.8 fusion.87
  10.7 8.9 %collective-permute-start.1 = (bf16[1,4,128,1024]{3,2,1,0:T(8,128)(2,1)}, bf16[1,4,128,1024]{3,2,1,0:T(8,128)(2,1)S(1)}, u32[]{:S(2)}, u32[]{:S(2)}) collective-permute-start(bf16[1,4,128,1024]{3,2,1,0:T(8,128)(2,1)} %get-tuple-element.31), channel_id=1, source_target_pairs={{0,62},{1,63},{2,0},{3,1},{4,2},{5,3},{6,4},{7,5},{8,6},{9,7},{10,... | collective-permute-start | bytes 3145736 | tf_op jit(solution)/shard_map/ppermute | solution.py:15
  19.6 3.2 collective-permute-start
  22.7 1.6 cosine_convert_fusion
  24.3 1.3 slice_bitcast_fusion.6
  25.6 16.1 %collective-permute-done.1 = bf16[1,4,128,1024]{3,2,1,0:T(8,128)(2,1)S(1)} collective-permute-done((bf16[1,4,128,1024]{3,2,1,0:T(8,128)(2,1)}, bf16[1,4,128,1024]{3,2,1,0:T(8,128)(2,1)S(1)}, u32[]{:S(2)}, u32[]{:S(2)}) %collective-permute-start.1) | collective-permute-done | bytes 1048608 | tf_op jit(solution)/shard_map/ppermute | solution.py:15
  41.7 0.2 convert_bitcast_fusion
  41.9 0.2 slice_bitcast_fusion.1
  42.2 0.3 copy.10
  42.5 1.3 copy.11
  43.8 20.4 %collective-permute-done = bf16[1,4,128,1024]{3,2,1,0:T(8,128)(2,1)} collective-permute-done((bf16[1,4,128,1024]{3,2,1,0:T(8,128)(2,1)}, bf16[1,4,128,1024]{3,2,1,0:T(8,128)(2,1)}, u32[]{:S(2)}, u32[]{:S(2)}) %collective-permute-start) | collective-permute-done | bytes 1048608 | tf_op jit(solution)/shard_map/ppermute | solution.py:15
  64.2 1.5 convert_bitcast_fusion.1
  65.6 1.2 slice_bitcast_fusion.3
  66.8 0.3 copy.8
  67.1 1.6 copy.9
  68.7 0.0 copy-start.14
  68.7 30.1 %add_reduce_fusion.4 = (bf16[32,512,128]{2,1,0:T(8,128)(2,1)}, bf16[32,512,128]{2,1,0:T(8,128)(2,1)}, bf16[32,512,128]{2,1,0:T(8,128)(2,1)S(1)}, bf16[32,512,128]{2,1,0:T(8,128)(2,1)S(1)}) fusion(f32[4,32,512]{2,1,0:T(8,128)} %get-tuple-element.39, f32[4,32,512]{2,1,0:T(8,128)} %get-tuple-element.34, f32[4,512,128]{2,1,0:T(8,128)S(1)} %copy.9, ...), kind=kLoop, calls=%fused_computation.9 | loop fusion | flops 125829120 | bytes 21495808 | tf_op jit(solution)/shard_map/reduce_sum | solution.py:32
  98.8 0.0 copy-done.14
  98.8 2.3 fusion.70
  101.1 69.3 %add_reduce_fusion.3 = (bf16[32,512,128]{2,1,0:T(8,128)(2,1)}, bf16[32,512,128]{2,1,0:T(8,128)(2,1)}, bf16[32,512,128]{2,1,0:T(8,128)(2,1)}, bf16[32,512,128]{2,...) fusion(f32[4,512,128]{2,1,0:T(8,128)} %copy.11, f32[4,512,128]{2,1,0:T(8,128)S(1)} %copy.10, ...), kind=kLoop, calls=%fused_computation.7 | loop fusion | flops 188743680 | bytes 28835840 | tf_op jit(solution)/shard_map/reduce_sum | solution.py:32
  170.4 0.0 copy-start.6
  170.4 0.0 copy-start.7
  170.4 5.0 %fusion.61 = bf16[32,101,128]{2,1,0:T(8,128)(2,1)S(1)} fusion(bf16[32,512,128]{2,1,0:T(8,128)(2,1)} %get-tuple-element.14, bf16[32,512,128]{2,1,0:T(8,128)(2,1)} %get-tuple-element.13, bf16[512,101]{0,1:T(8,128)(2,1)} %get-tuple-element.46, bf16[512,101]{0,1:T(8,128)(2,1)S(1)} %get-tuple-element.45), kind=kOutput, calls=%fused_computation.66 | convolution fusion | flops 865267712 | bytes 9422848 | tf_op jit(solution)/shard_map/ikj,kl->ilj/dot_general | solution.py:35
  175.5 0.0 copy-done.6
  175.5 0.9 copy-done.7
  176.4 0.0 copy-done.15
  176.4 0.0 copy-start.5
  176.4 1.6 fusion.64
  178.0 0.6 copy-done.4
  178.6 1.3 copy-done.5
  179.8 0.0 copy-start.13
  179.8 1.6 fusion.67
  181.4 0.0 copy-done.13
  181.4 3.4 %pad_maximum_fusion.1 = bf16[128,101,128]{2,1,0:T(8,128)(2,1)} fusion(bf16[32,101,128]{2,1,0:T(8,128)(2,1)S(1)} %copy-done.13, bf16[32,101,128]{2,1,0:T(8,128)(2,1)S(1)} %fusion.67, bf16[32,101,128]{2,1,0:T(8,128)(2,1)S(1)} %fusion.64, bf16[32,101,128]{2,1,0:T(8,128)(2,1)S(1)} %fusion.61), kind=kLoop, calls=%fused_computation.49 | loop fusion | flops 4964352 | bytes 6619136 | tf_op jit(solution)/shard_map/concatenate | solution.py:65
  184.8 0.0 reduce-scatter.5.cloned.1.call-update
  184.9 0.0 reduce-scatter.3.cloned.1.call-start
  184.9 0.0 copy-start.8
  184.9 0.0 copy-start.9
  184.9 0.0 copy-start.10
  184.9 0.0 copy-start.11
  184.9 5.9 %fusion.58 = bf16[32,101,128]{2,1,0:T(8,128)(2,1)} fusion(bf16[32,512,128]{2,1,0:T(8,128)(2,1)} %get-tuple-element.12, bf16[32,512,128]{2,1,0:T(8,128)(2,1)} %get-tuple-element.11, bf16[512,101]{0,1:T(8,128)(2,1)} %get-tuple-element.46, bf16[512,101]{0,1:T(8,128)(2,1)S(1)} %get-tuple-element.45), kind=kOutput, calls=%fused_computation.65 | convolution fusion | flops 865267712 | bytes 9422848 | tf_op jit(solution)/shard_map/ikj,kl->ilj/dot_general | solution.py:35
  190.8 0.0 copy-done.8
  190.9 0.0 copy-done.9
  190.9 0.0 copy-done.10
  190.9 0.0 copy-done.11
  190.9 68.4 %add_reduce_fusion.7 = (bf16[32,512,128]{2,1,0:T(8,128)(2,1)}, bf16[32,512,128]{2,1,0:T(8,128)(2,1)}, bf16[32,512,128]{2,1,0:T(8,128)(2,1)}, bf16[32,512,128]{2,...) fusion(f32[4,512,128]{2,1,0:T(8,128)S(1)} %copy.9, f32[4,32,512]{2,1,0:T(8,128)S(1)} %copy-done.11, ...), kind=kLoop, calls=%fused_computation.15 | loop fusion | flops 188743680 | bytes 28835840 | tf_op jit(solution)/shard_map/reduce_sum | solution.py:32
  259.3 5.0 %fusion.49 = bf16[32,101,128]{2,1,0:T(8,128)(2,1)S(1)} fusion(bf16[32,512,128]{2,1,0:T(8,128)(2,1)} %get-tuple-element.6, bf16[32,512,128]{2,1,0:T(8,128)(2,1)} %get-tuple-element.5, bf16[512,101]{0,1:T(8,128)(2,1)} %get-tuple-element.46, bf16[512,101]{0,1:T(8,128)(2,1)S(1)} %get-tuple-element.45), kind=kOutput, calls=%fused_computation.62 | convolution fusion | flops 865267712 | bytes 9422848 | tf_op jit(solution)/shard_map/ikj,kl->ilj/dot_general | solution.py:35
  264.3 0.0 copy-done.2
  264.3 0.9 copy-done.3
  265.2 0.0 copy-done.16
  265.2 1.6 fusion.52
  266.8 0.6 copy-done
  267.4 1.3 copy-done.1
  268.7 1.6 fusion.55
  270.3 0.0 copy-done.12
  270.3 3.4 %pad_maximum_fusion = bf16[128,101,128]{2,1,0:T(8,128)(2,1)} fusion(bf16[32,101,128]{2,1,0:T(8,128)(2,1)S(1)} %copy-done.12, bf16[32,101,128]{2,1,0:T(8,128)(2,1)S(1)} %fusion.55, bf16[32,101,128]{2,1,0:T(8,128)(2,1)S(1)} %fusion.52, bf16[32,101,128]{2,1,0:T(8,128)(2,1)S(1)} %fusion.49), kind=kLoop, calls=%fused_computation.48 | loop fusion | flops 4964352 | bytes 6619136 | tf_op jit(solution)/shard_map/concatenate | solution.py:65
  273.7 0.0 reduce-scatter.3.cloned.1.call-update
  273.7 0.0 reduce-scatter.5.cloned.1.call-done
  273.7 42.3 %reduce-scatter.3.cloned.1.call-done = bf16[32,101,128]{2,1,0:T(8,128)(2,1)} async-done(((bf16[128,101,128]{2,1,0:T(8,128)(2,1)}), bf16[32,101,128]{2,1,0:T(8,128)(2,1)}) %reduce-scatter.3.cloned.1.call-update) | async-done | bytes 827408 | tf_op jit(solution)/shard_map/reduce_scatter | solution.py:64
  316.0 1.6 fusion.32
  317.7 2.4 copy.12
  (9 shorter events, 0.0 us)
Async XLA Ops:
  6.5 267.2 %reduce-scatter.5.cloned.1.call-start = ((), (), s32[]{:S(2)}) async-start(), calls=%async_computation.3 | async-start | bytes 4259840 | tf_op jit(solution)/shard_map/reduce_scatter | solution.py:64
  10.7 31.0 %collective-permute-start.1 = (bf16[1,4,128,1024]{3,2,1,0:T(8,128)(2,1)}, bf16[1,4,128,1024]{3,2,1,0:T(8,128)(2,1)S(1)}, u32[]{:S(2)}, u32[]{:S(2)}) collective-permute-start(bf16[1,4,128,1024]{3,2,1,0:T(8,128)(2,1)} %get-tuple-element.31), channel_id=1, source_target_pairs={{0,62},{1,63},{2,0},{3,1},{4,2},{5,3},{6,4},{7,5},{8,6},{9,7},{10,... | collective-permute-start | bytes 3145736 | tf_op jit(solution)/shard_map/ppermute | solution.py:15
  19.6 44.6 %collective-permute-start = (bf16[1,4,128,1024]{3,2,1,0:T(8,128)(2,1)}, bf16[1,4,128,1024]{3,2,1,0:T(8,128)(2,1)}, u32[]{:S(2)}, u32[]{:S(2)}) collective-permute-start(bf16[1,4,128,1024]{3,2,1,0:T(8,128)(2,1)} %get-tuple-element.31), channel_id=1, source_target_pairs={{0,63},{1,0},{2,1},{3,2},{4,3},{5,4},{6,5},{7,6},{8,7},{9,8},{10,9... | collective-permute-start | bytes 3145736 | tf_op jit(solution)/shard_map/ppermute | solution.py:15
  68.7 30.1 %copy-start.14 = (bf16[512,101]{0,1:T(8,128)(2,1)S(1)}, bf16[512,101]{0,1:T(8,128)(2,1)}, u32[]{:S(2)}) copy-start(bf16[512,101]{0,1:T(8,128)(2,1)} %get-tuple-element.46) | copy-start | bytes 310276
  170.4 5.1 %copy-start.6 = (bf16[32,512,128]{2,1,0:T(8,128)(2,1)S(1)}, bf16[32,512,128]{2,1,0:T(8,128)(2,1)}, u32[]{:S(2)}) copy-start(bf16[32,512,128]{2,1,0:T(8,128)(2,1)} %get-tuple-element.25) | copy-start | bytes 12582916
  170.4 6.0 %copy-start.7 = (bf16[32,512,128]{2,1,0:T(8,128)(2,1)S(1)}, bf16[32,512,128]{2,1,0:T(8,128)(2,1)}, u32[]{:S(2)}) copy-start(bf16[32,512,128]{2,1,0:T(8,128)(2,1)} %get-tuple-element.26) | copy-start | bytes 12582916
  170.4 6.0 %copy-start.15 = (bf16[512,101]{0,1:T(8,128)(2,1)S(1)}, bf16[512,101]{0,1:T(8,128)(2,1)}, u32[]{:S(2)}) copy-start(bf16[512,101]{0,1:T(8,128)(2,1)} %get-tuple-element.46) | copy-start | bytes 310276
  176.4 2.2 copy-start.4
  176.4 3.5 %copy-start.5 = (bf16[32,512,128]{2,1,0:T(8,128)(2,1)S(1)}, bf16[32,512,128]{2,1,0:T(8,128)(2,1)}, u32[]{:S(2)}) copy-start(bf16[32,512,128]{2,1,0:T(8,128)(2,1)} %get-tuple-element.28) | copy-start | bytes 12582916
  179.8 1.6 copy-start.13
  184.9 131.2 %reduce-scatter.3.cloned.1.call-start = ((), (), s32[]{:S(2)}) async-start(), calls=%async_computation.2 | async-start | bytes 4259840 | tf_op jit(solution)/shard_map/reduce_scatter | solution.py:64
  184.9 5.9 %copy-start.8 = (f32[4,32,512]{2,1,0:T(8,128)S(1)}, f32[4,32,512]{2,1,0:T(8,128)}, u32[]{:S(2)}) copy-start(f32[4,32,512]{2,1,0:T(8,128)} %get-tuple-element.35) | copy-start | bytes 786436
  184.9 5.9 %copy-start.9 = (f32[4,32,512]{2,1,0:T(8,128)S(1)}, f32[4,32,512]{2,1,0:T(8,128)}, u32[]{:S(2)}) copy-start(f32[4,32,512]{2,1,0:T(8,128)} %get-tuple-element.36) | copy-start | bytes 786436
  184.9 5.9 %copy-start.10 = (f32[4,32,512]{2,1,0:T(8,128)S(1)}, f32[4,32,512]{2,1,0:T(8,128)}, u32[]{:S(2)}) copy-start(f32[4,32,512]{2,1,0:T(8,128)} %get-tuple-element.37) | copy-start | bytes 786436
  184.9 5.9 %copy-start.11 = (f32[4,32,512]{2,1,0:T(8,128)S(1)}, f32[4,32,512]{2,1,0:T(8,128)}, u32[]{:S(2)}) copy-start(f32[4,32,512]{2,1,0:T(8,128)} %get-tuple-element.38) | copy-start | bytes 786436
  259.3 5.1 %copy-start.2 = (bf16[32,512,128]{2,1,0:T(8,128)(2,1)S(1)}, bf16[32,512,128]{2,1,0:T(8,128)(2,1)}, u32[]{:S(2)}) copy-start(bf16[32,512,128]{2,1,0:T(8,128)(2,1)} %get-tuple-element.21) | copy-start | bytes 12582916
  259.3 6.0 %copy-start.3 = (bf16[32,512,128]{2,1,0:T(8,128)(2,1)S(1)}, bf16[32,512,128]{2,1,0:T(8,128)(2,1)}, u32[]{:S(2)}) copy-start(bf16[32,512,128]{2,1,0:T(8,128)(2,1)} %get-tuple-element.22) | copy-start | bytes 12582916
  259.3 6.0 %copy-start.16 = (bf16[512,101]{0,1:T(8,128)(2,1)S(1)}, bf16[512,101]{0,1:T(8,128)(2,1)}, u32[]{:S(2)}) copy-start(bf16[512,101]{0,1:T(8,128)(2,1)} %get-tuple-element.46) | copy-start | bytes 310276
  265.2 2.2 copy-start
  265.2 3.5 %copy-start.1 = (bf16[32,512,128]{2,1,0:T(8,128)(2,1)S(1)}, bf16[32,512,128]{2,1,0:T(8,128)(2,1)}, u32[]{:S(2)}) copy-start(bf16[32,512,128]{2,1,0:T(8,128)(2,1)} %get-tuple-element.24) | copy-start | bytes 12582916
  268.7 1.6 copy-start.12
Sparse Core Ops, SparseCore 0:
  185.0 42.1 reduce-scatter.4
  273.8 42.1 reduce-scatter.2
where the time goes:
time: 329 us; the launch traced here: 327 us
  other arithmetic  184 us (56%)
  waiting for transfers between devices  78.8 us (24%)
  matrix products  24.7 us (8%)
  local copies, waits for them, and re-layouts  14.1 us (4%)
  between operations  13.6 us (4%)
  starting transfers between devices  12.1 us (4%)
    reduce_sum x3, other arithmetic, correlate(): real_part = jnp.sum(own_real * far_real + own_imag * far_imag, axis=(0, 1))  168 us
    reduce_scatter x2, waiting for transfers between devices, local(): lax.psum_scatter(jnp.concatenate(pieces, 0).astype(jnp.bfloat16), 'seg',...  42.3 us
    ppermute x2, waiting for transfers between devices, passed_along(): return lax.ppermute(value, axis, pairs)  36.4 us
    dot_general x8, matrix products, correlate(): jnp.einsum('ikj,kl->ilj', spectrum, table, preferred_element_type=jnp.flo...  24.7 us
    ppermute x2, starting transfers between devices, passed_along(): return lax.ppermute(value, axis, pairs)  12 us
    concatenate x2, other arithmetic, local(): jnp.concatenate(pieces, 0).astype(jnp.bfloat16)  6.75 us
  transfers between devices with their start and end apart: 4, of which 3 were waited for; matrix products, arithmetic and copies ran while one was open for 28% of the time, Pallas kernels for 0%

commit v1 on v0

v1 whole, which is shorter than its diff:
```python
import functools
import math

import jax
import jax.numpy as jnp
import ml_dtypes
import numpy as np
from jax import lax
from jax.experimental import pallas as pl
from jax.experimental.pallas import tpu as pltpu
from jax.sharding import PartitionSpec as P

MESH = pl.DeviceIdType.MESH
ROUNDS = 2
LAGS = 101
LAG_ROWS = 112
SEGS = 4
WIN = 4
CB = 128
F = 512
HALF_F = F // 2
GROUPS = HALF_F // 8
PER_STEP = 2
STEPS = GROUPS // PER_STEP
BURST = 8
ROWS = CB // 2
OUT_ROWS = CB // SEGS
AHEAD = 2
LAG_F2 = 2
LAG_F1 = 4
LAG_C = 5
PIECES = 4


def lag_table(core):
    f = core * HALF_F + np.arange(HALF_F, dtype=np.int64).reshape(GROUPS, 1, 8)
    t = np.arange(LAGS, dtype=np.int64).reshape(LAGS, 1, 1, 1) - (LAGS - 1) // 2
    phase = np.mod(f * t, 2 * F) * (math.pi / F)
    both = np.concatenate([np.cos(phase), -np.sin(phase)], 2).reshape(LAGS, GROUPS * 16)
    return np.pad(both, ((0, LAG_ROWS - LAGS), (0, 0)))


def shortcut(step):
    return lax.rem(step, 3) == 1


def kernel(n_chan, spectra, valid, table, out, staged, own, far, other, turned, left, cross, acc, sums, landed,
           in_sem, s_own, r_own, s_z, r_z, s_x, r_x, s_fz, r_fz, s_fx, r_fx, s_sum, r_sum):
    seg = lax.axis_index("seg")
    chan = lax.axis_index("chan")
    core = lax.rem(seg, 2)
    x_lo = seg // 2
    x_hi = lax.rem(chan, 2)
    sibling = (seg + 1 - 2 * core, chan)
    pair_near = (lax.rem(seg + 2, SEGS), chan)
    pair_cross = (SEGS - 1 - seg, chan)
    below = (seg, lax.rem(chan + n_chan - 2, n_chan))
    above = (seg, lax.rem(chan + 2, n_chan))
    across = (lax.rem(seg + 2, SEGS), chan + 1 - 2 * x_hi)
    near0 = 2 * x_lo
    away0 = 2 - near0

    barrier = pltpu.get_barrier_semaphore()
    for device in (sibling, pair_near, pair_cross, above, across):
        pl.semaphore_signal(barrier, inc=1, device_id=device, device_id_type=MESH)

    def load(block):
        half = lax.rem(core + block // 2, 2)
        first = half * HALF_F + lax.rem(block, 2) * 128
        copies = []
        for part in range(2):
            source = pl.multiple_of(first + part * F, 128)
            copies.append(pltpu.make_async_copy(
                spectra.at[0, :, :, pl.ds(source, 128)],
                staged.at[block, part],
                in_sem.at[block, part],
            ))
        return copies

    for block in (0, 2, 1, 3):
        for copy in load(block):
            copy.start()

    counts = valid[...]
    inverse = 1.0 / jnp.sqrt(counts.astype(jnp.float32))
    weights = [jnp.where(w < counts, inverse, 0.0) for w in range(WIN)]

    def prepare(block):
        for copy in load(block):
            copy.wait()
        for part in range(2):
            for pair in range(2):
                rows = [
                    (staged[block, part, 2 * pair + k].T * weights[2 * pair + k]).reshape(16, 8, CB)
                    for k in range(2)
                ]
                both = jnp.concatenate(rows, 1).astype(jnp.bfloat16)
                groups = pl.ds(16 * (block % 2), 16)
                place = pl.ds(part * 32 + pair * 16, 16)
                if block < 2:
                    own[seg, groups, place, :] = both
                else:
                    other[groups, place, :] = both

    def groups_of(step):
        return pl.ds(step * PER_STEP, PER_STEP)

    def own_copies(step):
        g = groups_of(step)
        mine = own.at[seg, g]
        theirs = other.at[g]
        target = own.at[seg, g]
        return [
            pltpu.make_async_remote_copy(mine, target, s_own.at[0, step], r_own.at[0, step], pair_near, MESH),
            pltpu.make_async_remote_copy(theirs, target, s_own.at[1, step], r_own.at[1, step], pair_cross, MESH),
            pltpu.make_async_remote_copy(theirs, target, s_own.at[2, step], r_own.at[2, step], sibling, MESH),
        ]

    def z_copy(step, short):
        segs = pl.ds(near0, 2) if short else pl.ds(0, SEGS)
        g = groups_of(step)
        return pltpu.make_async_remote_copy(
            own.at[segs, g], far.at[1, segs, g], s_z.at[step], r_z.at[step], below, MESH)

    def x_copy(step, short, send, from_far):
        segs = pl.ds(near0 if send else away0, 2) if short else pl.ds(0, SEGS)
        g = groups_of(step)
        source = far.at[1, segs, g] if from_far else own.at[segs, g]
        return pltpu.make_async_remote_copy(
            source, far.at[0, segs, g], s_x.at[step], r_x.at[step], across, MESH)

    def fz_copy(step, send):
        segs = pl.ds(near0 if send else away0, 2)
        piece = far.at[1, segs, groups_of(step)]
        return pltpu.make_async_remote_copy(piece, piece, s_fz.at[step], r_fz.at[step], pair_near, MESH)

    def fx_copy(step, send):
        segs = pl.ds(away0 if send else near0, 2)
        piece = far.at[0, segs, groups_of(step)]
        return pltpu.make_async_remote_copy(piece, piece, s_fx.at[step], r_fx.at[step], pair_near, MESH)

    def by_kind(step, act):
        short = shortcut(step)

        @pl.when(short)
        def _():
            act(True)

        @pl.when(jnp.logical_not(short))
        def _():
            act(False)

    def send_own(step):
        for copy in own_copies(step):
            copy.start()

    def stage_own(step):
        for copy in own_copies(step):
            copy.wait_recv()

        def act(short):
            z_copy(step, short).start()

            @pl.when(x_hi == 1)
            def _():
                x_copy(step, short, True, False).start()

        by_kind(step, act)

    def stage_z(step):
        def act(short):
            z_copy(step, short).wait_recv()

            @pl.when(x_hi == 0)
            def _():
                x_copy(step, short, True, True).start()

            if short:
                fz_copy(step, True).start()

        by_kind(step, act)

    def stage_x(step):
        def act(short):
            x_copy(step, short, False, False).wait_recv()
            if short:
                fx_copy(step, True).start()

        by_kind(step, act)

    lane = lax.broadcasted_iota(jnp.int32, (8, 128), 1)
    row = lax.broadcasted_iota(jnp.int32, (8, 128), 0)
    mask = (lax.rem(lane, 8) == row).astype(jnp.float32)
    base = x_lo * ROWS

    def spectrum(step):
        for k in range(PER_STEP):
            group = step * PER_STEP + k
            for part in range(2):
                rows = pl.ds(part * 32, 32)
                picked = jnp.concatenate([own[s, group, rows, :] for s in range(SEGS)], 0)
                turned[part] = picked.astype(jnp.float32).T
            for i in range(ROWS):
                u = turned[0, pl.ds(base + i, 1), :] * mask
                v = turned[1, pl.ds(base + i, 1), :] * mask
                left[pl.ds(i * 16, 16), 0:128] = jnp.concatenate([u, v], 0).astype(jnp.bfloat16)
                left[pl.ds(i * 16, 16), 128:256] = jnp.concatenate([v, -u], 0).astype(jnp.bfloat16)
            right = jnp.concatenate(
                [
                    jnp.concatenate(
                        [far[r, s, group, pl.ds(part * 32, 32), :] for part in range(2) for s in range(SEGS)], 0
                    )
                    for r in range(ROUNDS)
                ],
                1,
            )
            product = jnp.dot(left[...], right, preferred_element_type=jnp.float32)
            spot = pl.multiple_of(lax.rem(group, BURST) * 16, 16)
            cross[:, pl.ds(spot, 16), :] = product.reshape(ROWS, 16, ROUNDS * CB).astype(jnp.bfloat16)

    def projected(burst, i):
        columns = pl.ds(pl.multiple_of(burst * BURST * 16, BURST * 16), BURST * 16)
        return jnp.dot(table[core, :, columns], cross[i], preferred_element_type=jnp.float32)

    def stage_compute(step):
        @pl.when(shortcut(step))
        def _():
            fz_copy(step, False).wait_recv()
            fx_copy(step, False).wait_recv()

        spectrum(step)
        burst = step // (BURST // PER_STEP)

        @pl.when(jnp.logical_and(lax.rem(step, BURST // PER_STEP) == BURST // PER_STEP - 1, step < STEPS - 1))
        def _():
            @pl.loop(0, ROWS)
            def _(i):
                term = projected(burst, i)

                @pl.when(burst == 0)
                def _():
                    acc[i] = term

                @pl.when(burst > 0)
                def _():
                    acc[i] = acc[i] + term

    prepare(0)
    prepare(2)
    pl.semaphore_wait(barrier, 5)
    for step in range(AHEAD):
        send_own(step)
    prepare(1)
    prepare(3)

    @pl.loop(0, STEPS + LAG_C)
    def _(t):
        @pl.when(t + AHEAD < STEPS)
        def _():
            send_own(t + AHEAD)

        @pl.when(t < STEPS)
        def _():
            stage_own(t)

        @pl.when(jnp.logical_and(t >= LAG_F2, t < STEPS + LAG_F2))
        def _():
            stage_z(t - LAG_F2)

        @pl.when(jnp.logical_and(t >= LAG_F1, t < STEPS + LAG_F1))
        def _():
            stage_x(t - LAG_F1)

        @pl.when(t >= LAG_C)
        def _():
            stage_compute(t - LAG_C)

    per_piece = OUT_ROWS // PIECES
    last = GROUPS // BURST - 1

    def sum_copy(piece):
        rows = pl.ds(piece * per_piece, per_piece)
        return pltpu.make_async_remote_copy(
            sums.at[rows], landed.at[rows], s_sum.at[piece], r_sum.at[piece], sibling, MESH)

    for piece in range(PIECES):
        @pl.loop(0, per_piece)
        def _(k):
            q = piece * per_piece + k
            i = (1 - core) * OUT_ROWS + q
            sums[q] = (acc[i] + projected(last, i)).astype(jnp.bfloat16)

        sum_copy(piece).start()

    scale = 1.0 / math.sqrt(F * SEGS)
    for piece in range(PIECES):
        @pl.loop(0, per_piece)
        def _(k):
            i = core * OUT_ROWS + piece * per_piece + k
            acc[i] = acc[i] + projected(last, i)

    for piece in range(PIECES):
        sum_copy(piece).wait_recv()

        @pl.loop(0, per_piece)
        def _(k):
            q = piece * per_piece + k
            i = core * OUT_ROWS + q
            total = (acc[i] + landed[q].astype(jnp.float32)) * scale
            for r in range(ROUNDS):
                out[r, q] = total[:LAGS, r * CB:(r + 1) * CB]

    @pl.loop(0, STEPS)
    def _(step):
        for copy in own_copies(step):
            copy.wait_send()

        def act(short):
            z_copy(step, short).wait_send()
            x_copy(step, short, True, False).wait_send()
            if short:
                fz_copy(step, True).wait_send()
                fx_copy(step, True).wait_send()

        by_kind(step, act)

    for piece in range(PIECES):
        sum_copy(piece).wait_send()


def local(n_chan, table, spectra, valid):
    stacked = pl.pallas_call(
        functools.partial(kernel, n_chan),
        name="correlate",
        out_shape=jax.ShapeDtypeStruct((ROUNDS, OUT_ROWS, LAGS, CB), jnp.float32),
        in_specs=[
            pl.BlockSpec(memory_space=pl.ANY),
            pl.BlockSpec(memory_space=pltpu.VMEM),
            pl.BlockSpec(memory_space=pltpu.VMEM),
        ],
        out_specs=pl.BlockSpec(memory_space=pltpu.VMEM),
        scratch_shapes=[
            pltpu.VMEM((4, 2, WIN, CB, 128), jnp.float32),
            pltpu.VMEM((SEGS, GROUPS, 64, CB), jnp.bfloat16),
            pltpu.VMEM((ROUNDS, SEGS, GROUPS, 64, CB), jnp.bfloat16),
            pltpu.VMEM((GROUPS, 64, CB), jnp.bfloat16),
            pltpu.VMEM((2, CB, 128), jnp.float32),
            pltpu.VMEM((ROWS * 16, 256), jnp.bfloat16),
            pltpu.VMEM((ROWS, BURST * 16, ROUNDS * CB), jnp.bfloat16),
            pltpu.VMEM((ROWS, LAG_ROWS, ROUNDS * CB), jnp.float32),
            pltpu.VMEM((OUT_ROWS, LAG_ROWS, ROUNDS * CB), jnp.bfloat16),
            pltpu.VMEM((OUT_ROWS, LAG_ROWS, ROUNDS * CB), jnp.bfloat16),
            pltpu.SemaphoreType.DMA((4, 2)),
            pltpu.SemaphoreType.DMA((3, STEPS)),
            pltpu.SemaphoreType.DMA((3, STEPS)),
            pltpu.SemaphoreType.DMA((STEPS,)),
            pltpu.SemaphoreType.DMA((STEPS,)),
            pltpu.SemaphoreType.DMA((STEPS,)),
            pltpu.SemaphoreType.DMA((STEPS,)),
            pltpu.SemaphoreType.DMA((STEPS,)),
            pltpu.SemaphoreType.DMA((STEPS,)),
            pltpu.SemaphoreType.DMA((STEPS,)),
            pltpu.SemaphoreType.DMA((STEPS,)),
            pltpu.SemaphoreType.DMA((PIECES,)),
            pltpu.SemaphoreType.DMA((PIECES,)),
        ],
        compiler_params=pltpu.CompilerParams(
            collective_id=0, has_side_effects=True, vmem_limit_bytes=56 * 2**20),
    )(spectra, valid, table)
    return stacked[:, None]


def solution(mesh):
    n_chan = mesh.shape["chan"]

    def run(spectra, valid):
        table = jnp.asarray(np.stack([lag_table(0), lag_table(1)]).astype(ml_dtypes.bfloat16))
        return jax.shard_map(
            functools.partial(local, n_chan, table),
            mesh=mesh,
            in_specs=(P("seg", None, "chan", None), P("seg", "chan")),
            out_specs=P(None, "chan", "seg", None, None),
            check_vma=False,
        )(spectra, valid)

    return run
```

time: 329 us -> 103 us (0.31)
  the two profiles are of different devices: /device:TPU:1 before, /device:TPU:100 now
where the time goes in v1:
time: 103 us; the launch traced here: 102 us
  Pallas kernels  98.2 us (95%)
  local copies, waits for them, and re-layouts  4.32 us (4%)
    pallas_call x1, Pallas kernels, local(): pl.pallas_call(functools.partial(kernel, n_chan), name='correlate', out_s...  98.2 us
    broadcast_in_dim x1, local copies, waits for them, and re-layouts, local(): return stacked[:, None]  4.32 us

profile of v1, /device:TPU:100, one launch (start us, length us, event | category | flops | bytes accessed | tf_op | source)
XLA Modules:
  0.0 102.5 jit_solution(10378333981876294907)
XLA Ops:
  0.0 98.2 %correlate.1 = f32[2,32,101,128]{3,2,1,0:T(8,128)} custom-call(f32[1,4,128,1024]{3,2,1,0:T(8,128)} %spectra.1, s32[1,128]{1,0:T(1,128)} %valid.1, bf16[2,112,512]{2,1,0:T(8,128)(2,1)} %constant.2.clone.table), custom_call_target="tpu_custom_call" | custom-call | tf_op jit(solution)/shard_map/correlate/pallas_call | solution.py:332
  98.2 4.3 %copy.4 = f32[2,1,32,101,128]{4,2,3,1,0:T(8,128)} copy(f32[2,1,32,101,128]{4,3,2,0,1:T(8,128)} %bitcast.1) | data formatting | bytes 6619136 | tf_op jit(solution)/shard_map/broadcast_in_dim | solution.py:370

commit v2 on v1

--- a/solution.py
+++ b/solution.py
@@ -30,6 +30,8 @@
 LAG_F1 = 4
 LAG_C = 5
 PIECES = 4
+LAG_BLOCK = 56
+UNROLL = 8
 
 
 def lag_table(core):
@@ -44,8 +46,8 @@
     return lax.rem(step, 3) == 1
 
 
-def kernel(n_chan, spectra, valid, table, out, staged, own, far, other, turned, left, cross, acc, sums, landed,
-           in_sem, s_own, r_own, s_z, r_z, s_x, r_x, s_fz, r_fz, s_fx, r_fx, s_sum, r_sum):
+def kernel(n_chan, spectra, valid_in, table_in, kept, landed, valid, table, staged, own, far, other, turned, left, cross, acc, sums,
+           in_sem, small_sem, s_own, r_own, s_z, r_z, s_x, r_x, s_fz, r_fz, s_fx, r_fx, s_sum, r_sum):
     seg = lax.axis_index("seg")
     chan = lax.axis_index("chan")
     core = lax.rem(seg, 2)
@@ -77,10 +79,15 @@
             ))
         return copies
 
+    valid_copy = pltpu.make_async_copy(valid_in, valid, small_sem.at[0])
+    table_copy = pltpu.make_async_copy(table_in.at[core], table, small_sem.at[1])
+    valid_copy.start()
     for block in (0, 2, 1, 3):
         for copy in load(block):
             copy.start()
 
+    table_copy.start()
+    valid_copy.wait()
     counts = valid[...]
     inverse = 1.0 / jnp.sqrt(counts.astype(jnp.float32))
     weights = [jnp.where(w < counts, inverse, 0.0) for w in range(WIN)]
@@ -220,7 +227,7 @@
 
     def projected(burst, i):
         columns = pl.ds(pl.multiple_of(burst * BURST * 16, BURST * 16), BURST * 16)
-        return jnp.dot(table[core, :, columns], cross[i], preferred_element_type=jnp.float32)
+        return jnp.dot(table[:, columns], cross[i], preferred_element_type=jnp.float32)
 
     def stage_compute(step):
         @pl.when(shortcut(step))
@@ -233,17 +240,21 @@
 
         @pl.when(jnp.logical_and(lax.rem(step, BURST // PER_STEP) == BURST // PER_STEP - 1, step < STEPS - 1))
         def _():
-            @pl.loop(0, ROWS)
-            def _(i):
-                term = projected(burst, i)
-
-                @pl.when(burst == 0)
-                def _():
-                    acc[i] = term
-
-                @pl.when(burst > 0)
-                def _():
-                    acc[i] = acc[i] + term
+            @pl.when(burst == 0)
+            def _():
+                @pl.loop(0, ROWS // UNROLL)
+                def _(first):
+                    for k in range(UNROLL):
+                        i = first * UNROLL + k
+                        acc[i] = projected(burst, i)
+
+            @pl.when(burst > 0)
+            def _():
+                @pl.loop(0, ROWS // UNROLL)
+                def _(first):
+                    for k in range(UNROLL):
+                        i = first * UNROLL + k
+                        acc[i] = acc[i] + projected(burst, i)
 
     prepare(0)
     prepare(2)
@@ -252,6 +263,7 @@
         send_own(step)
     prepare(1)
     prepare(3)
+    table_copy.wait()
 
     @pl.loop(0, STEPS + LAG_C)
     def _(t):
@@ -284,31 +296,21 @@
             sums.at[rows], landed.at[rows], s_sum.at[piece], r_sum.at[piece], sibling, MESH)
 
     for piece in range(PIECES):
-        @pl.loop(0, per_piece)
-        def _(k):
+        for k in range(per_piece):
             q = piece * per_piece + k
             i = (1 - core) * OUT_ROWS + q
             sums[q] = (acc[i] + projected(last, i)).astype(jnp.bfloat16)
-
         sum_copy(piece).start()
 
-    scale = 1.0 / math.sqrt(F * SEGS)
-    for piece in range(PIECES):
-        @pl.loop(0, per_piece)
-        def _(k):
-            i = core * OUT_ROWS + piece * per_piece + k
-            acc[i] = acc[i] + projected(last, i)
+    @pl.loop(0, OUT_ROWS // UNROLL)
+    def _(first):
+        for k in range(UNROLL):
+            q = first * UNROLL + k
+            i = core * OUT_ROWS + q
+            kept[q] = acc[i] + projected(last, i)
 
     for piece in range(PIECES):
         sum_copy(piece).wait_recv()
-
-        @pl.loop(0, per_piece)
-        def _(k):
-            q = piece * per_piece + k
-            i = core * OUT_ROWS + q
-            total = (acc[i] + landed[q].astype(jnp.float32)) * scale
-            for r in range(ROUNDS):
-                out[r, q] = total[:LAGS, r * CB:(r + 1) * CB]
 
     @pl.loop(0, STEPS)
     def _(step):
@@ -328,18 +330,35 @@
         sum_copy(piece).wait_send()
 
 
+def finish(kept, landed, out):
+    scale = 1.0 / math.sqrt(F * SEGS)
+    lanes = pl.ds(pl.multiple_of(pl.program_id(0) * CB, CB), CB)
+    lags = pl.ds(pl.multiple_of(pl.program_id(1) * LAG_BLOCK, LAG_BLOCK), LAG_BLOCK)
+    for i in range(0, OUT_ROWS, 8):
+        rows = pl.ds(i, 8)
+        total = (kept[rows, lags, lanes] + landed[rows, lags, lanes].astype(jnp.float32)) * scale
+        total = jnp.swapaxes(total, 0, 1)
+        for lag in range(LAG_BLOCK):
+            out[0, pl.ds(lag * OUT_ROWS + i, 8), :] = total[lag]
+
+
 def local(n_chan, table, spectra, valid):
-    stacked = pl.pallas_call(
+    kept, landed = pl.pallas_call(
         functools.partial(kernel, n_chan),
         name="correlate",
-        out_shape=jax.ShapeDtypeStruct((ROUNDS, OUT_ROWS, LAGS, CB), jnp.float32),
+        out_shape=[
+            pltpu.VMEM((OUT_ROWS, LAG_ROWS, ROUNDS * CB), jnp.float32),
+            pltpu.VMEM((OUT_ROWS, LAG_ROWS, ROUNDS * CB), jnp.bfloat16),
+        ],
         in_specs=[
-            pl.BlockSpec(memory_space=pl.ANY),
-            pl.BlockSpec(memory_space=pltpu.VMEM),
-            pl.BlockSpec(memory_space=pltpu.VMEM),
+            pl.BlockSpec(memory_space=pltpu.HBM),
+            pl.BlockSpec(memory_space=pltpu.HBM),
+            pl.BlockSpec(memory_space=pltpu.HBM),
         ],
-        out_specs=pl.BlockSpec(memory_space=pltpu.VMEM),
+        out_specs=[pl.BlockSpec(memory_space=pltpu.VMEM)] * 2,
         scratch_shapes=[
+            pltpu.VMEM((1, CB), jnp.int32),
+            pltpu.VMEM((LAG_ROWS, GROUPS * 16), jnp.bfloat16),
             pltpu.VMEM((4, 2, WIN, CB, 128), jnp.float32),
             pltpu.VMEM((SEGS, GROUPS, 64, CB), jnp.bfloat16),
             pltpu.VMEM((ROUNDS, SEGS, GROUPS, 64, CB), jnp.bfloat16),
@@ -349,8 +368,8 @@
             pltpu.VMEM((ROWS, BURST * 16, ROUNDS * CB), jnp.bfloat16),
             pltpu.VMEM((ROWS, LAG_ROWS, ROUNDS * CB), jnp.float32),
             pltpu.VMEM((OUT_ROWS, LAG_ROWS, ROUNDS * CB), jnp.bfloat16),
-            pltpu.VMEM((OUT_ROWS, LAG_ROWS, ROUNDS * CB), jnp.bfloat16),
             pltpu.SemaphoreType.DMA((4, 2)),
+            pltpu.SemaphoreType.DMA((2,)),
             pltpu.SemaphoreType.DMA((3, STEPS)),
             pltpu.SemaphoreType.DMA((3, STEPS)),
             pltpu.SemaphoreType.DMA((STEPS,)),
@@ -365,9 +384,19 @@
             pltpu.SemaphoreType.DMA((PIECES,)),
         ],
         compiler_params=pltpu.CompilerParams(
-            collective_id=0, has_side_effects=True, vmem_limit_bytes=56 * 2**20),
-    )(spectra, valid, table)
-    return stacked[:, None]
+            collective_id=0, has_side_effects=True, vmem_limit_bytes=32 * 2**20),
+    )(*(pltpu.with_memory_space_constraint(x, pltpu.HBM) for x in (spectra, valid, table)))
+    whole = pl.BlockSpec(memory_space=pltpu.VMEM)
+    stacked = pl.pallas_call(
+        finish,
+        name="finish",
+        grid=(ROUNDS, LAG_ROWS // LAG_BLOCK),
+        out_shape=jax.ShapeDtypeStruct((ROUNDS, LAGS * OUT_ROWS, CB), jnp.float32),
+        in_specs=[whole, whole],
+        out_specs=pl.BlockSpec((1, LAG_BLOCK * OUT_ROWS, CB), lambda r, l: (r, l, 0)),
+        compiler_params=pltpu.CompilerParams(vmem_limit_bytes=16 * 2**20),
+    )(pltpu.with_memory_space_constraint(kept, pltpu.VMEM), pltpu.with_memory_space_constraint(landed, pltpu.VMEM))
+    return stacked.reshape(ROUNDS, 1, LAGS, OUT_ROWS, CB).transpose(0, 1, 3, 2, 4)
 
 
 def solution(mesh):

time: 103 us -> 68.6 us (0.67)
  the two profiles are of different devices: /device:TPU:100 before, /device:TPU:1 now
where the time goes in v2:
time: 68.6 us; the launch traced here: 67.3 us
  Pallas kernels  67.3 us (98%)
    pallas_call x1, Pallas kernels, local(): pl.pallas_call(functools.partial(kernel, n_chan), name='correlate', out_s...  64.7 us
    pallas_call x1, Pallas kernels, local(): pl.pallas_call(finish, name='finish', grid=(ROUNDS, LAG_ROWS // LAG_BLOCK...  2.62 us

profile of v2, /device:TPU:1, one launch (start us, length us, event | category | flops | bytes accessed | tf_op | source)
XLA Modules:
  0.0 67.3 jit_solution(7176696710182046777)
XLA Ops:
  0.0 64.7 %correlate.1 = (f32[32,112,256]{2,1,0:T(8,128)S(1)}, bf16[32,112,256]{2,1,0:T(8,128)(2,1)S(1)}) custom-call(f32[1,4,128,1024]{3,2,1,0:T(8,128)} %spectra.1, s32[1,128]{1,0:T(1,128)} %valid_in.1, bf16[2,112,512]{2,1,0:T(8,128)(2,1)} %constant.2.clone.table_in), custom_call_target="tpu_custom_call" | custom-call | tf_op jit(solution)/shard_map/correlate/pallas_call | solution.py:346
  64.7 2.6 %finish.1 = f32[2,3232,128]{2,1,0:T(8,128)} custom-call(f32[32,112,256]{2,1,0:T(8,128)S(1)} %get-tuple-element.7.kept, bf16[32,112,256]{2,1,0:T(8,128)(2,1)S(1)} %get-tuple-element.8.landed), custom_call_target="tpu_custom_call" | custom-call | tf_op jit(solution)/shard_map/finish/pallas_call | solution.py:390

commit v3 on v2

v3 whole, which is shorter than its diff:
```python
import functools
import math

import jax
import jax.numpy as jnp
import ml_dtypes
import numpy as np
from jax import lax
from jax.experimental import pallas as pl
from jax.experimental.pallas import tpu as pltpu
from jax.sharding import PartitionSpec as P

MESH = pl.DeviceIdType.MESH
ROUNDS = 2
LAGS = 101
LAG_ROWS = 112
SEGS = 4
WIN = 4
CB = 128
F = 512
HALF_F = F // 2
GROUPS = HALF_F // 8
PER_STEP = 2
STEPS = GROUPS // PER_STEP
BURST = 8
ROWS = CB // 2
OUT_ROWS = CB // SEGS
HALF = CB // 2
AHEAD = 2
LAG_F2 = 2
LAG_F1 = 4
LAG_C = 6
PIECES = 4
LAG_BLOCK = 56
UNROLL = 8


def lag_table(core):
    f = core * HALF_F + np.arange(HALF_F, dtype=np.int64).reshape(GROUPS, 1, 8)
    t = np.arange(LAGS, dtype=np.int64).reshape(LAGS, 1, 1, 1) - (LAGS - 1) // 2
    phase = np.mod(f * t, 2 * F) * (math.pi / F)
    both = np.concatenate([np.cos(phase), -np.sin(phase)], 2).reshape(LAGS, GROUPS * 16)
    return np.pad(both, ((0, LAG_ROWS - LAGS), (0, 0)))


def kernel(n_chan, spectra, valid_in, table_in, kept, landed, valid, table, staged, own, far, other, turned, left, cross, acc, sums,
           in_sem, small_sem, s_own, r_own, s_z, r_z, s_x, r_x, s_f, r_f, s_sum, r_sum):
    seg = lax.axis_index("seg")
    chan = lax.axis_index("chan")
    core = lax.rem(seg, 2)
    x_lo = seg // 2
    x_hi = lax.rem(chan, 2)
    sibling = (seg + 1 - 2 * core, chan)
    pair_near = (lax.rem(seg + 2, SEGS), chan)
    pair_cross = (SEGS - 1 - seg, chan)
    below = (seg, lax.rem(chan + n_chan - 2, n_chan))
    above = (seg, lax.rem(chan + 2, n_chan))
    across = (lax.rem(seg + 2, SEGS), chan + 1 - 2 * x_hi)
    near = pl.ds(2 * x_lo, 2)
    away = pl.ds(2 - 2 * x_lo, 2)

    barrier = pltpu.get_barrier_semaphore()
    for device in (sibling, pair_near, pair_cross, above, across):
        pl.semaphore_signal(barrier, inc=1, device_id=device, device_id_type=MESH)

    def load(block):
        half = lax.rem(core + block // 2, 2)
        first = half * HALF_F + lax.rem(block, 2) * 128
        copies = []
        for part in range(2):
            source = pl.multiple_of(first + part * F, 128)
            copies.append(pltpu.make_async_copy(
                spectra.at[0, :, :, pl.ds(source, 128)],
                staged.at[block, part],
                in_sem.at[block, part],
            ))
        return copies

    valid_copy = pltpu.make_async_copy(valid_in, valid, small_sem.at[0])
    table_copy = pltpu.make_async_copy(table_in.at[core], table, small_sem.at[1])
    valid_copy.start()
    for block in (0, 2, 1, 3):
        for copy in load(block):
            copy.start()

    table_copy.start()
    valid_copy.wait()
    first_half = lax.broadcasted_iota(jnp.int32, (8, 8, CB), 2) < HALF
    counts = valid[...]
    inverse = 1.0 / jnp.sqrt(counts.astype(jnp.float32))
    weights = [jnp.where(w < counts, inverse, 0.0) for w in range(WIN)]

    def prepare(block):
        for copy in load(block):
            copy.wait()
        steps = pl.ds(8 * (block % 2), 8)
        for part in range(2):
            for pair in range(2):
                lows, highs = [], []
                for w in (2 * pair, 2 * pair + 1):
                    rows = (staged[block, part, w].T * weights[w]).reshape(8, 2, 8, CB)
                    even = rows[:, 0]
                    odd = pltpu.roll(rows[:, 1].reshape(64, CB), HALF, 1).reshape(8, 8, CB)
                    lows.append(jnp.where(first_half, even, odd))
                    highs.append(jnp.where(first_half, odd, even))
                place = pl.ds(part * 32 + pair * 16, 16)
                for half, both in enumerate((lows, highs)):
                    both = jnp.concatenate(both, 1).astype(jnp.bfloat16)
                    if block < 2:
                        own[seg, steps, half, place, :] = both
                    else:
                        other[steps, half, place, :] = both

    def own_copies(step):
        half = 1 - x_lo
        target = own.at[seg, step, half]
        return [
            pltpu.make_async_remote_copy(
                own.at[seg, step, half], target, s_own.at[0, step], r_own.at[0, step], pair_near, MESH),
            pltpu.make_async_remote_copy(
                other.at[step, half], target, s_own.at[1, step], r_own.at[1, step], pair_cross, MESH),
            pltpu.make_async_remote_copy(
                other.at[step], own.at[seg, step], s_own.at[2, step], r_own.at[2, step], sibling, MESH),
        ]

    def own_arrivals(step):
        def arrival(kind, place):
            return pltpu.make_async_remote_copy(
                place, place, s_own.at[kind, step], r_own.at[kind, step], sibling, MESH)

        return [
            arrival(0, own.at[pair_near[0], step, x_lo]),
            arrival(1, own.at[pair_cross[0], step, x_lo]),
            arrival(2, own.at[sibling[0], step]),
        ]

    def z_copy(step, part):
        if part == 0:
            source, target = own.at[near, step], far.at[1, near, step]
        else:
            source, target = own.at[away, step, x_lo], far.at[1, away, step, x_lo]
        return pltpu.make_async_remote_copy(source, target, s_z.at[part, step], r_z.at[part, step], below, MESH)

    def x_copy(step, part, from_far):
        segs = near if part == 0 else away
        place = (segs, step) if part == 0 else (segs, step, x_lo)
        source = far.at[(1,) + place] if from_far else own.at[place]
        return pltpu.make_async_remote_copy(
            source, far.at[(0,) + place], s_x.at[part, step], r_x.at[part, step], across, MESH)

    def x_arrival(step, part):
        place = far.at[0, away, step] if part == 0 else far.at[0, near, step, 1 - x_lo]
        return pltpu.make_async_remote_copy(place, place, s_x.at[part, step], r_x.at[part, step], across, MESH)

    def pair_copy(step, which, send):
        if which == 1:
            place = far.at[1, near if send else away, step, x_lo if send else 1 - x_lo]
        else:
            place = far.at[0, away if send else near, step, 1 - x_lo if send else x_lo]
        return pltpu.make_async_remote_copy(place, place, s_f.at[which, step], r_f.at[which, step], pair_near, MESH)

    def send_own(step):
        for copy in own_copies(step):
            copy.start()

    def stage_own(step):
        arrivals = own_arrivals(step)
        arrivals[2].wait_recv()
        z_copy(step, 0).start()

        @pl.when(x_hi == 1)
        def _():
            x_copy(step, 0, False).start()

        arrivals[0].wait_recv()
        arrivals[1].wait_recv()
        z_copy(step, 1).start()

        @pl.when(x_hi == 1)
        def _():
            x_copy(step, 1, False).start()

    def stage_z(step):
        z_copy(step, 0).wait_recv()
        pair_copy(step, 1, True).start()

        @pl.when(x_hi == 0)
        def _():
            x_copy(step, 0, True).start()

        z_copy(step, 1).wait_recv()

        @pl.when(x_hi == 0)
        def _():
            x_copy(step, 1, True).start()

    def stage_x(step):
        x_arrival(step, 0).wait_recv()
        pair_copy(step, 0, True).start()
        x_arrival(step, 1).wait_recv()

    lane = lax.broadcasted_iota(jnp.int32, (8, 128), 1)
    row = lax.broadcasted_iota(jnp.int32, (8, 128), 0)
    low_lanes = lax.broadcasted_iota(jnp.int32, (256, CB), 1) < HALF
    mask = (lax.rem(lane, 8) == row).astype(jnp.float32)

    def spectrum(step, k):
        if k == 0:
            for part in range(2):
                rows = pl.ds(part * 32, 32)
                picked = jnp.concatenate([own[s, step, x_lo, rows, :] for s in range(SEGS)], 0)
                turned[part] = picked.astype(jnp.float32).T
        base = ROWS * lax.rem(k + x_lo, 2)
        for i in range(ROWS):
            u = turned[0, pl.ds(base + i, 1), :] * mask
            v = turned[1, pl.ds(base + i, 1), :] * mask
            left[pl.ds(i * 16, 16), 0:128] = jnp.concatenate([u, v], 0).astype(jnp.bfloat16)
            left[pl.ds(i * 16, 16), 128:256] = jnp.concatenate([v, -u], 0).astype(jnp.bfloat16)
        blocks = []
        for r in range(ROUNDS):
            low, high = [
                jnp.concatenate(
                    [far[r, s, step, half, pl.ds(part * 32, 32), :] for part in range(2) for s in range(SEGS)], 0
                ).astype(jnp.float32)
                for half in range(2)
            ]
            if k == 0:
                block = jnp.where(low_lanes, low, high)
            else:
                block = pltpu.roll(jnp.where(low_lanes, high, low), HALF, 1)
            blocks.append(block.astype(jnp.bfloat16))
        right = jnp.concatenate(blocks, 1)
        product = jnp.dot(left[...], right, preferred_element_type=jnp.float32)
        group = step * PER_STEP + k
        spot = pl.multiple_of(lax.rem(group, BURST) * 16, 16)
        slot = lax.rem(group // BURST, 2)
        cross[slot, :, pl.ds(spot, 16), :] = product.reshape(ROWS, 16, ROUNDS * CB).astype(jnp.bfloat16)

    def projected(burst, i):
        columns = pl.ds(pl.multiple_of(burst * BURST * 16, BURST * 16), BURST * 16)
        slot = burst % 2 if isinstance(burst, int) else lax.rem(burst, 2)
        return jnp.dot(table[:, columns], cross[slot, i], preferred_element_type=jnp.float32)

    per_burst = BURST // PER_STEP
    share = ROWS // per_burst

    def project_share(step):
        burst = step // per_burst - 1
        first = lax.rem(step, per_burst) * share

        @pl.when(burst == 0)
        def _():
            for k in range(share):
                acc[first + k] = projected(burst, first + k)

        @pl.when(burst > 0)
        def _():
            for k in range(share):
                acc[first + k] = acc[first + k] + projected(burst, first + k)

    prepare(0)
    prepare(2)
    pl.semaphore_wait(barrier, 5)
    for step in range(AHEAD):
        send_own(step)
    prepare(1)
    prepare(3)
    table_copy.wait()

    @pl.loop(0, STEPS + LAG_C)
    def _(t):
        @pl.when(t + AHEAD < STEPS)
        def _():
            send_own(t + AHEAD)

        @pl.when(t < STEPS)
        def _():
            stage_own(t)

        @pl.when(t >= LAG_C)
        def _():
            pair_copy(t - LAG_C, 1, False).wait_recv()
            pair_copy(t - LAG_C, 0, False).wait_recv()
            spectrum(t - LAG_C, 0)

        @pl.when(jnp.logical_and(t >= LAG_F2, t < STEPS + LAG_F2))
        def _():
            stage_z(t - LAG_F2)

        @pl.when(t >= LAG_C)
        def _():
            spectrum(t - LAG_C, 1)

        @pl.when(jnp.logical_and(t >= LAG_F1, t < STEPS + LAG_F1))
        def _():
            stage_x(t - LAG_F1)

        @pl.when(t >= LAG_C + per_burst)
        def _():
            project_share(t - LAG_C)

    per_piece = OUT_ROWS // PIECES
    last = GROUPS // BURST - 1

    def sum_copy(piece):
        rows = pl.ds(piece * per_piece, per_piece)
        return pltpu.make_async_remote_copy(
            sums.at[rows], landed.at[rows], s_sum.at[piece], r_sum.at[piece], sibling, MESH)

    for piece in range(PIECES):
        for k in range(per_piece):
            q = piece * per_piece + k
            i = (1 - core) * OUT_ROWS + q
            sums[q] = (acc[i] + projected(last, i)).astype(jnp.bfloat16)
        sum_copy(piece).start()

    @pl.loop(0, OUT_ROWS // UNROLL)
    def _(first):
        for k in range(UNROLL):
            q = first * UNROLL + k
            i = core * OUT_ROWS + q
            kept[q] = acc[i] + projected(last, i)

    for piece in range(PIECES):
        sum_copy(piece).wait_recv()

    @pl.loop(0, STEPS)
    def _(step):
        for copy in own_copies(step):
            copy.wait_send()

        for part in range(2):
            z_copy(step, part).wait_send()
            x_copy(step, part, False).wait_send()
            pair_copy(step, part, True).wait_send()

    for piece in range(PIECES):
        sum_copy(piece).wait_send()


def finish(kept, landed, out):
    scale = 1.0 / math.sqrt(F * SEGS)
    lanes = pl.ds(pl.multiple_of(pl.program_id(0) * CB, CB), CB)
    lags = pl.ds(pl.multiple_of(pl.program_id(1) * LAG_BLOCK, LAG_BLOCK), LAG_BLOCK)
    for i in range(0, OUT_ROWS, 8):
        rows = pl.ds(i, 8)
        total = (kept[rows, lags, lanes] + landed[rows, lags, lanes].astype(jnp.float32)) * scale
        total = jnp.swapaxes(total, 0, 1)
        for lag in range(LAG_BLOCK):
            out[0, pl.ds(lag * OUT_ROWS + i, 8), :] = total[lag]


def local(n_chan, table, spectra, valid):
    kept, landed = pl.pallas_call(
        functools.partial(kernel, n_chan),
        name="correlate",
        out_shape=[
            pltpu.VMEM((OUT_ROWS, LAG_ROWS, ROUNDS * CB), jnp.float32),
            pltpu.VMEM((OUT_ROWS, LAG_ROWS, ROUNDS * CB), jnp.bfloat16),
        ],
        in_specs=[
            pl.BlockSpec(memory_space=pltpu.HBM),
            pl.BlockSpec(memory_space=pltpu.HBM),
            pl.BlockSpec(memory_space=pltpu.HBM),
        ],
        out_specs=[pl.BlockSpec(memory_space=pltpu.VMEM)] * 2,
        scratch_shapes=[
            pltpu.VMEM((1, CB), jnp.int32),
            pltpu.VMEM((LAG_ROWS, GROUPS * 16), jnp.bfloat16),
            pltpu.VMEM((4, 2, WIN, CB, 128), jnp.float32),
            pltpu.VMEM((SEGS, STEPS, 2, 64, CB), jnp.bfloat16),
            pltpu.VMEM((ROUNDS, SEGS, STEPS, 2, 64, CB), jnp.bfloat16),
            pltpu.VMEM((STEPS, 2, 64, CB), jnp.bfloat16),
            pltpu.VMEM((2, CB, 128), jnp.float32),
            pltpu.VMEM((ROWS * 16, 256), jnp.bfloat16),
            pltpu.VMEM((2, ROWS, BURST * 16, ROUNDS * CB), jnp.bfloat16),
            pltpu.VMEM((ROWS, LAG_ROWS, ROUNDS * CB), jnp.float32),
            pltpu.VMEM((OUT_ROWS, LAG_ROWS, ROUNDS * CB), jnp.bfloat16),
            pltpu.SemaphoreType.DMA((4, 2)),
            pltpu.SemaphoreType.DMA((2,)),
            pltpu.SemaphoreType.DMA((3, STEPS)),
            pltpu.SemaphoreType.DMA((3, STEPS)),
            pltpu.SemaphoreType.DMA((2, STEPS)),
            pltpu.SemaphoreType.DMA((2, STEPS)),
            pltpu.SemaphoreType.DMA((2, STEPS)),
            pltpu.SemaphoreType.DMA((2, STEPS)),
            pltpu.SemaphoreType.DMA((2, STEPS)),
            pltpu.SemaphoreType.DMA((2, STEPS)),
            pltpu.SemaphoreType.DMA((PIECES,)),
            pltpu.SemaphoreType.DMA((PIECES,)),
        ],
        compiler_params=pltpu.CompilerParams(
            collective_id=0, has_side_effects=True, vmem_limit_bytes=32 * 2**20),
    )(*(pltpu.with_memory_space_constraint(x, pltpu.HBM) for x in (spectra, valid, table)))
    whole = pl.BlockSpec(memory_space=pltpu.VMEM)
    stacked = pl.pallas_call(
        finish,
        name="finish",
        grid=(ROUNDS, LAG_ROWS // LAG_BLOCK),
        out_shape=jax.ShapeDtypeStruct((ROUNDS, LAGS * OUT_ROWS, CB), jnp.float32),
        in_specs=[whole, whole],
        out_specs=pl.BlockSpec((1, LAG_BLOCK * OUT_ROWS, CB), lambda r, l: (r, l, 0)),
        compiler_params=pltpu.CompilerParams(vmem_limit_bytes=16 * 2**20),
    )(pltpu.with_memory_space_constraint(kept, pltpu.VMEM), pltpu.with_memory_space_constraint(landed, pltpu.VMEM))
    return stacked.reshape(ROUNDS, 1, LAGS, OUT_ROWS, CB).transpose(0, 1, 3, 2, 4)


def solution(mesh):
    n_chan = mesh.shape["chan"]

    def run(spectra, valid):
        table = jnp.asarray(np.stack([lag_table(0), lag_table(1)]).astype(ml_dtypes.bfloat16))
        return jax.shard_map(
            functools.partial(local, n_chan, table),
            mesh=mesh,
            in_specs=(P("seg", None, "chan", None), P("seg", "chan")),
            out_specs=P(None, "chan", "seg", None, None),
            check_vma=False,
        )(spectra, valid)

    return run
```

time: 68.6 us -> 62.9 us (0.917); the launches traced: 67.3 us -> 62.8 us
  Pallas kernels: 67.3 us -> 62.8 us
    pallas_call x1, Pallas kernels: 64.7 us -> 60.2 us  [local(): pl.pallas_call(functools.partial(kernel, n_chan), name='correlate', out_s...]
where the time goes in v3:
time: 62.9 us; the launch traced here: 62.8 us
  Pallas kernels  62.8 us (100%)
    pallas_call x1, Pallas kernels, local(): pl.pallas_call(functools.partial(kernel, n_chan), name='correlate', out_s...  60.2 us
    pallas_call x1, Pallas kernels, local(): pl.pallas_call(finish, name='finish', grid=(ROUNDS, LAG_ROWS // LAG_BLOCK...  2.62 us

profile of v3, /device:TPU:1, one launch (start us, length us, event | category | flops | bytes accessed | tf_op | source)
XLA Modules:
  0.0 62.8 jit_solution(3998547938393468084)
XLA Ops:
  0.0 60.2 %correlate.1 = (f32[32,112,256]{2,1,0:T(8,128)S(1)}, bf16[32,112,256]{2,1,0:T(8,128)(2,1)S(1)}) custom-call(f32[1,4,128,1024]{3,2,1,0:T(8,128)} %spectra.1, s32[1,128]{1,0:T(1,128)} %valid_in.1, bf16[2,112,512]{2,1,0:T(8,128)(2,1)} %constant.2.clone.table_in), custom_call_target="tpu_custom_call" | custom-call | tf_op jit(solution)/shard_map/correlate/pallas_call | solution.py:354
  60.2 2.6 %finish.1 = f32[2,3232,128]{2,1,0:T(8,128)} custom-call(f32[32,112,256]{2,1,0:T(8,128)S(1)} %get-tuple-element.7.kept, bf16[32,112,256]{2,1,0:T(8,128)(2,1)S(1)} %get-tuple-element.8.landed), custom_call_target="tpu_custom_call" | custom-call | tf_op jit(solution)/shard_map/finish/pallas_call | solution.py:396

commit v4 on v3

--- a/solution.py
+++ b/solution.py
@@ -28,10 +28,12 @@
 HALF = CB // 2
 AHEAD = 2
 LAG_F2 = 2
-LAG_F1 = 4
-LAG_C = 6
+LAG_F1 = 3
+LAG_C = 5
+Z_SIZE = 8
+Z_DELAY = 1
 PIECES = 4
-LAG_BLOCK = 56
+LAG_BLOCK = 16
 UNROLL = 8
 
 
@@ -44,7 +46,7 @@
 
 
 def kernel(n_chan, spectra, valid_in, table_in, kept, landed, valid, table, staged, own, far, other, turned, left, cross, acc, sums,
-           in_sem, small_sem, s_own, r_own, s_z, r_z, s_x, r_x, s_f, r_f, s_sum, r_sum):
+           in_sem, small_sem, s_own, r_own, s_z, r_z, s_x, r_x, s_f, r_f, s_sum, r_sum, z_ready):
     seg = lax.axis_index("seg")
     chan = lax.axis_index("chan")
     core = lax.rem(seg, 2)
@@ -60,7 +62,8 @@
     away = pl.ds(2 - 2 * x_lo, 2)
 
     barrier = pltpu.get_barrier_semaphore()
-    for device in (sibling, pair_near, pair_cross, above, across):
+    late = lax.rem(chan // 2, Z_SIZE) == 0
+    for device in (sibling, pair_near, pair_cross, below, across):
         pl.semaphore_signal(barrier, inc=1, device_id=device, device_id_type=MESH)
 
     def load(block):
@@ -166,7 +169,14 @@
     def stage_own(step):
         arrivals = own_arrivals(step)
         arrivals[2].wait_recv()
-        z_copy(step, 0).start()
+
+        @pl.when(jnp.logical_and(step == 0, jnp.logical_not(late)))
+        def _():
+            pl.semaphore_wait(z_ready, 1)
+
+        @pl.when(jnp.logical_not(late))
+        def _():
+            z_copy(step, 0).start()
 
         @pl.when(x_hi == 1)
         def _():
@@ -174,7 +184,10 @@
 
         arrivals[0].wait_recv()
         arrivals[1].wait_recv()
-        z_copy(step, 1).start()
+
+        @pl.when(jnp.logical_not(late))
+        def _():
+            z_copy(step, 1).start()
 
         @pl.when(x_hi == 1)
         def _():
@@ -261,6 +274,7 @@
     prepare(0)
     prepare(2)
     pl.semaphore_wait(barrier, 5)
+    pl.semaphore_signal(z_ready, inc=1, device_id=above, device_id_type=MESH)
     for step in range(AHEAD):
         send_own(step)
     prepare(1)
@@ -276,6 +290,15 @@
         @pl.when(t < STEPS)
         def _():
             stage_own(t)
+
+        @pl.when(jnp.logical_and(late, t == Z_DELAY))
+        def _():
+            pl.semaphore_wait(z_ready, 1)
+
+        @pl.when(jnp.logical_and(late, jnp.logical_and(t >= Z_DELAY, t < STEPS + Z_DELAY)))
+        def _():
+            z_copy(t - Z_DELAY, 0).start()
+            z_copy(t - Z_DELAY, 1).start()
 
         @pl.when(t >= LAG_C)
         def _():
@@ -338,16 +361,35 @@
         sum_copy(piece).wait_send()
 
 
-def finish(kept, landed, out):
+def finish(kept, landed, out, turned, sems):
     scale = 1.0 / math.sqrt(F * SEGS)
-    lanes = pl.ds(pl.multiple_of(pl.program_id(0) * CB, CB), CB)
-    lags = pl.ds(pl.multiple_of(pl.program_id(1) * LAG_BLOCK, LAG_BLOCK), LAG_BLOCK)
-    for i in range(0, OUT_ROWS, 8):
-        rows = pl.ds(i, 8)
-        total = (kept[rows, lags, lanes] + landed[rows, lags, lanes].astype(jnp.float32)) * scale
-        total = jnp.swapaxes(total, 0, 1)
-        for lag in range(LAG_BLOCK):
-            out[0, pl.ds(lag * OUT_ROWS + i, 8), :] = total[lag]
+    blocks = LAG_ROWS // LAG_BLOCK
+    block_rows = LAG_BLOCK * OUT_ROWS
+    last_rows = LAGS * OUT_ROWS - (blocks - 1) * block_rows
+
+    def leave(n, act):
+        r, block = n // blocks, lax.rem(n, blocks)
+        for rows, here in ((block_rows, block < blocks - 1), (last_rows, block == blocks - 1)):
+            @pl.when(here)
+            def _():
+                start = pl.multiple_of(block * block_rows, 8)
+                act(pltpu.make_async_copy(turned.at[n, pl.ds(0, rows)], out.at[r, pl.ds(start, rows)], sems.at[n]))
+
+    @pl.loop(0, ROUNDS * blocks)
+    def _(n):
+        lanes = pl.ds(pl.multiple_of(n // blocks * CB, CB), CB)
+        lags = pl.ds(pl.multiple_of(lax.rem(n, blocks) * LAG_BLOCK, LAG_BLOCK), LAG_BLOCK)
+        for i in range(0, OUT_ROWS, 8):
+            rows = pl.ds(i, 8)
+            total = (kept[rows, lags, lanes] + landed[rows, lags, lanes].astype(jnp.float32)) * scale
+            total = jnp.swapaxes(total, 0, 1)
+            for lag in range(LAG_BLOCK):
+                turned[n, pl.ds(lag * OUT_ROWS + i, 8), :] = total[lag]
+        leave(n, lambda copy: copy.start())
+
+    @pl.loop(0, ROUNDS * blocks)
+    def _(n):
+        leave(n, lambda copy: copy.wait())
 
 
 def local(n_chan, table, spectra, valid):
@@ -388,18 +430,22 @@
             pltpu.SemaphoreType.DMA((2, STEPS)),
             pltpu.SemaphoreType.DMA((PIECES,)),
             pltpu.SemaphoreType.DMA((PIECES,)),
+            pltpu.SemaphoreType.REGULAR,
         ],
         compiler_params=pltpu.CompilerParams(
             collective_id=0, has_side_effects=True, vmem_limit_bytes=32 * 2**20),
     )(*(pltpu.with_memory_space_constraint(x, pltpu.HBM) for x in (spectra, valid, table)))
-    whole = pl.BlockSpec(memory_space=pltpu.VMEM)
+    in_vmem = pl.BlockSpec(memory_space=pltpu.VMEM)
     stacked = pl.pallas_call(
         finish,
         name="finish",
-        grid=(ROUNDS, LAG_ROWS // LAG_BLOCK),
         out_shape=jax.ShapeDtypeStruct((ROUNDS, LAGS * OUT_ROWS, CB), jnp.float32),
-        in_specs=[whole, whole],
-        out_specs=pl.BlockSpec((1, LAG_BLOCK * OUT_ROWS, CB), lambda r, l: (r, l, 0)),
+        in_specs=[in_vmem, in_vmem],
+        out_specs=pl.BlockSpec(memory_space=pltpu.HBM),
+        scratch_shapes=[
+            pltpu.VMEM((ROUNDS * (LAG_ROWS // LAG_BLOCK), LAG_BLOCK * OUT_ROWS, CB), jnp.float32),
+            pltpu.SemaphoreType.DMA((ROUNDS * (LAG_ROWS // LAG_BLOCK),)),
+        ],
         compiler_params=pltpu.CompilerParams(vmem_limit_bytes=16 * 2**20),
     )(pltpu.with_memory_space_constraint(kept, pltpu.VMEM), pltpu.with_memory_space_constraint(landed, pltpu.VMEM))
     return stacked.reshape(ROUNDS, 1, LAGS, OUT_ROWS, CB).transpose(0, 1, 3, 2, 4)

time: 62.9 us -> 60.5 us (0.962)
  the two profiles are of different devices: /device:TPU:1 before, /device:TPU:253 now
where the time goes in v4:
time: 60.5 us; the launch traced here: 60.4 us
  Pallas kernels  60.4 us (100%)
    pallas_call x1, Pallas kernels, local(): pl.pallas_call(functools.partial(kernel, n_chan), name='correlate', out_s...  58.4 us
    pallas_call x1, Pallas kernels, local(): pl.pallas_call(finish, name='finish', out_shape=jax.ShapeDtypeStruct((ROU...  1.99 us

profile of v4, /device:TPU:253, one launch (start us, length us, event | category | flops | bytes accessed | tf_op | source)
XLA Modules:
  0.0 60.4 jit_solution(52309095950674132)
XLA Ops:
  0.0 58.4 %correlate.1 = (f32[32,112,256]{2,1,0:T(8,128)S(1)}, bf16[32,112,256]{2,1,0:T(8,128)(2,1)S(1)}) custom-call(f32[1,4,128,1024]{3,2,1,0:T(8,128)} %spectra.1, s32[1,128]{1,0:T(1,128)} %valid_in.1, bf16[2,112,512]{2,1,0:T(8,128)(2,1)} %constant.2.clone.table_in), custom_call_target="tpu_custom_call" | custom-call | tf_op jit(solution)/shard_map/correlate/pallas_call | solution.py:396
  58.4 2.0 %finish.1 = f32[2,3232,128]{2,1,0:T(8,128)} custom-call(f32[32,112,256]{2,1,0:T(8,128)S(1)} %get-tuple-element.7.kept, bf16[32,112,256]{2,1,0:T(8,128)(2,1)S(1)} %get-tuple-element.8.landed), custom_call_target="tpu_custom_call" | custom-call | tf_op jit(solution)/shard_map/finish/pallas_call | solution.py:439

commit v5 on v4

--- a/solution.py
+++ b/solution.py
@@ -287,10 +287,6 @@
         def _():
             send_own(t + AHEAD)
 
-        @pl.when(t < STEPS)
-        def _():
-            stage_own(t)
-
         @pl.when(jnp.logical_and(late, t == Z_DELAY))
         def _():
             pl.semaphore_wait(z_ready, 1)
@@ -299,6 +295,10 @@
         def _():
             z_copy(t - Z_DELAY, 0).start()
             z_copy(t - Z_DELAY, 1).start()
+
+        @pl.when(t < STEPS)
+        def _():
+            stage_own(t)
 
         @pl.when(t >= LAG_C)
         def _():

time: 60.5 us -> 60.5 us (level)
  the two profiles are of different devices: /device:TPU:253 before, /device:TPU:1 now
where the time goes in v5:
time: 60.5 us; the launch traced here: 59.7 us
  Pallas kernels  59.7 us (99%)
    pallas_call x1, Pallas kernels, local(): pl.pallas_call(functools.partial(kernel, n_chan), name='correlate', out_s...  57.7 us
    pallas_call x1, Pallas kernels, local(): pl.pallas_call(finish, name='finish', out_shape=jax.ShapeDtypeStruct((ROU...  1.99 us

profile of v5, /device:TPU:1, one launch (start us, length us, event | category | flops | bytes accessed | tf_op | source)
XLA Modules:
  0.0 59.7 jit_solution(1305430181822964282)
XLA Ops:
  0.0 57.7 %correlate.1 = (f32[32,112,256]{2,1,0:T(8,128)S(1)}, bf16[32,112,256]{2,1,0:T(8,128)(2,1)S(1)}) custom-call(f32[1,4,128,1024]{3,2,1,0:T(8,128)} %spectra.1, s32[1,128]{1,0:T(1,128)} %valid_in.1, bf16[2,112,512]{2,1,0:T(8,128)(2,1)} %constant.2.clone.table_in), custom_call_target="tpu_custom_call" | custom-call | tf_op jit(solution)/shard_map/correlate/pallas_call | solution.py:396
  57.7 2.0 %finish.1 = f32[2,3232,128]{2,1,0:T(8,128)} custom-call(f32[32,112,256]{2,1,0:T(8,128)S(1)} %get-tuple-element.7.kept, bf16[32,112,256]{2,1,0:T(8,128)(2,1)S(1)} %get-tuple-element.8.landed), custom_call_target="tpu_custom_call" | custom-call | tf_op jit(solution)/shard_map/finish/pallas_call | solution.py:439
